TPU v7x, 256 devices: a whole 4x4x8 slice. The times are simulated.
256 devices in a mesh: dp: 8 (over z), expert: 32 (over x, y, core).
Axes of the slice: x: 4, y: 4, z: 8, core: 2. Of those that a mesh axis runs over, the one named last changes fastest.
Arguments:
- tokens: bfloat16 [32768, 2048], P(('dp', 'expert')), parts along dimension 0, may hold values from -6 to 6
- routes: int32 [32768, 8], P(('dp', 'expert')), parts along dimension 0, may hold values from 0 to 31, all different within a row; in each aligned block of 128 rows (0 to 127, 128 to 255, ...) at most 40 rows name the same one
- gate_num: int32 [32768, 8], P(('dp', 'expert')), parts along dimension 0, may hold values from 1 to 1023
- w_gate: bfloat16 [32, 2048, 768], P('expert'), may hold values from -0.125 to 0.125
- w_up: bfloat16 [32, 2048, 768], P('expert'), may hold values from -0.125 to 0.125
- w_down: bfloat16 [32, 768, 2048], P('expert'), may hold values from -0.21875 to 0.21875
Outputs:
- combined: bfloat16 [32768, 2048], P(('dp', 'expert')), parts along dimension 0
There are 8 independent parts, one for each index of `dp`. A program takes and returns all parts, laid end to end along the dimension named above; an argument that names none is the same for every part. Nothing has to cross between parts.
Inputs may be any that keep to these rules, and one draw needn't show every extreme that they name: `routes`: each row names 8 different experts; among the rows of one device no expert is named more than 40 times, a bound that some block reaches.
All inputs are finite; a program needn't handle non-finite values.
Results may differ from a plain program's by a relative error of at most 0.0057.
Values may be sent and summed in bfloat16 or wider, within the bound.
No kernel may reach another device: no remote copies, remote signals or barrier semaphores. Data moves between devices by JAX's collectives and lax.ppermute only.
A program may use at most 128 MiB of HBM per device.

v0:
```python
import jax
import jax.numpy as jnp
from jax import lax
from jax.sharding import PartitionSpec as P

GATE_DEN = 1024


def expert_apply(rows, w_gate, w_up, w_down):
    gate_part = jnp.einsum("srd,dh->srh", rows, w_gate[0], preferred_element_type=jnp.float32)
    up_part = jnp.einsum("srd,dh->srh", rows, w_up[0], preferred_element_type=jnp.float32)
    hidden = (jax.nn.silu(gate_part) * up_part).astype(jnp.bfloat16)
    return jnp.einsum("srh,hd->srd", hidden, w_down[0], preferred_element_type=jnp.float32).astype(
        jnp.bfloat16
    )


def send_back(outputs):
    return lax.all_to_all(outputs, "expert", split_axis=0, concat_axis=0, tiled=True)


def body(tokens, routes, gate_num, w_gate, w_up, w_down):
    group_size = lax.axis_size("expert")
    tok_dev = tokens.shape[0]
    top_count = routes.shape[1]
    capacity = min(tok_dev, 5 * tok_dev * top_count // (4 * group_size))
    expert_range = jnp.arange(group_size, dtype=jnp.int32)
    slot_range = jnp.arange(capacity, dtype=jnp.int32)
    onehot = jnp.any(routes[:, :, None] == expert_range[None, None, :], axis=1).astype(jnp.int32)
    slots = jnp.cumsum(onehot, axis=0) - 1
    all_rows = lax.all_gather(tokens, "expert", axis=0, tiled=True)
    all_routes = lax.all_gather(routes, "expert", axis=0, tiled=True)
    own_expert = lax.axis_index("expert")
    routed = (
        jnp.any(all_routes == own_expert, axis=1).astype(jnp.int32).reshape(group_size, tok_dev)
    )
    all_slots = jnp.cumsum(routed, axis=1) - 1
    selector = (
        (routed[:, None, :] == 1) & (all_slots[:, None, :] == slot_range[None, :, None])
    ).astype(jnp.bfloat16)
    grouped = all_rows.reshape(group_size, tok_dev, all_rows.shape[1])
    buffer = jnp.einsum(
        "sct,std->scd", selector, grouped, preferred_element_type=jnp.float32
    ).astype(jnp.bfloat16)
    returned = send_back(expert_apply(buffer, w_gate, w_up, w_down))
    returned_flat = returned.reshape(group_size * capacity, returned.shape[2])
    slot_chosen = jnp.take_along_axis(slots, routes, axis=1)
    flat_slot = routes * capacity + slot_chosen
    picked = returned_flat[flat_slot]
    weights = gate_num.astype(jnp.float32) / GATE_DEN
    combined = jnp.sum(picked.astype(jnp.float32) * weights[:, :, None], axis=1)
    return combined.astype(jnp.bfloat16)


def solution(mesh):
    placed = (
        P(("dp", "expert"), None),
        P(("dp", "expert"), None),
        P(("dp", "expert"), None),
        P("expert", None, None),
        P("expert", None, None),
        P("expert", None, None),
    )
    return jax.shard_map(
        body, mesh=mesh, in_specs=placed, out_specs=P(("dp", "expert"), None), check_vma=False
    )
```

profile of v0, /device:TPU:8, one launch (start us, length us, event | category | flops | bytes accessed | tf_op | source)
XLA Modules:
  0.0 225.0 jit_solution(1968779918979069390)
XLA Ops:
  6.5 0.0 copy-start
  6.5 0.0 all-gather.2.cloned.1.call-start
  6.5 0.7 all-gather.2.cloned.1.call-update
  7.3 24.6 %all_gather.6 = s32[4096,8]{0,1:T(8,128)S(1)} all-gather(s32[128,8]{0,1:T(8,128)} %param.7), channel_id=1, replica_groups=mesh['dp'=8,'expert'=32] {'expert'}, dimensions={0}, use_global_device_ids=true | all-gather | bytes 135168 | tf_op jit(solution)/shard_map/all_gather | solution.py:32
  31.9 0.1 compare_reduce_fusion
  31.9 0.3 reduce_window_sum.22
  32.3 57.7 %all-gather.2.cloned.1.call-done = bf16[4096,2048]{1,0:T(8,128)(2,1)} async-done(((bf16[128,2048]{1,0:T(8,128)(2,1)}), bf16[4096,2048]{1,0:T(8,128)(2,1)}) %all-gather.2.cloned.1.call-update) | async-done | bytes 16777232 | tf_op jit(solution)/shard_map/all_gather | solution.py:31
  90.0 0.0 copy-start.4
  90.0 8.2 %convolution_convert_fusion.1 = bf16[32,40,2048]{2,1,0:T(8,128)(2,1)S(1)} fusion(bf16[32,128,2048]{2,1,0:T(8,128)(2,1)} %bitcast.32, s32[32,128]{1,0:T(8,128)S(1)} %broadcast_add_fusion.1, pred[32,128]{1,0:T(8,128)(4,1)S(1)} %broadcast_compare_fusion), kind=kOutput, calls=%fused_computation.5 | convolution fusion | flops 674037760 | bytes 22040576 | tf_op jit(solution)/shard_map/sct,std->scd/dot_general | solution.py:42
  98.2 0.0 copy-start.1
  98.2 2.3 %copy-done.1 = bf16[32,40,2048]{2,1,0:T(8,128)(2,1)} copy-done((bf16[32,40,2048]{2,1,0:T(8,128)(2,1)}, bf16[32,40,2048]{2,1,0:T(8,128)(2,1)S(1)}, u32[]{:S(2)}) %copy-start.1) | copy-done | bytes 5242904
  100.6 0.0 copy-done.4
  100.6 6.4 %fusion.2 = f32[32,40,768]{2,1,0:T(8,128)} fusion(bf16[32,40,2048]{2,1,0:T(8,128)(2,1)S(1)} %convolution_convert_fusion.1, bf16[1,2048,768]{2,1,0:T(8,128)(2,1)S(1)} %copy-done.4), kind=kOutput, calls=%fused_computation.8 | convolution fusion | flops 4026531840 | bytes 12320768 | tf_op jit(solution)/shard_map/srd,dh->srh/dot_general | solution.py:11
  107.0 0.0 copy-done
  107.0 14.7 %convolution_convert_fusion = bf16[32,40,2048]{2,1,0:T(8,128)(2,1)} fusion(bf16[1,768,2048]{2,1,0:T(8,128)(2,1)S(1)} %copy-done, f32[32,40,768]{2,1,0:T(8,128)} %fusion.2, bf16[32,40,2048]{2,1,0:T(8,128)(2,1)} %copy-done.1, bf16[1,2048,768]{2,1,0:T(8,128)(2,1)} %param.9), kind=kOutput, calls=%fused_computation.4 | convolution fusion | flops 8061583360 | bytes 20709376 | tf_op jit(solution)/shard_map/srh,hd->srd/dot_general | solution.py:13
  121.7 0.0 copy-start.2
  121.7 6.2 %all-to-all-start = ((bf16[32,40,2048]{2,1,0:T(8,128)(2,1)}), bf16[32,40,2048]{2,1,0:T(8,128)(2,1)}, u32[]{:S(2)}, u32[]{:S(2)}) async-start(bf16[32,40,2048]{2,1,0:T(8,128)(2,1)} %convolution_convert_fusion), calls=%async_computation | async-start | bytes 10485760 | tf_op jit(solution)/shard_map/all_to_all | solution.py:19
  128.0 0.0 copy-done.2
  128.0 0.1 copy.27
  128.1 0.2 reduce_window_sum.23
  128.3 0.1 copy.28
  128.4 0.1 reshape.53
  128.5 0.0 copy-start.3
  128.5 7.1 %gather_fusion.1 = s32[1024]{0:T(1024)S(1)} fusion(s32[128,32]{1,0:T(8,128)S(1)} %broadcast_add_fusion, s32[1024]{0:T(1024)S(1)} %reshape.53), kind=kCustom, calls=%fused_computation.1 | custom fusion | bytes 16384 | tf_op jit(solution)/shard_map/jit(take_along_axis)/gather | solution.py:47
  135.6 0.1 reshape.56
  135.7 0.1 copy.30
  135.9 0.1 reshape.47
  136.0 0.0 copy-done.3
  136.0 0.1 copy.31
  136.1 62.8 %all-to-all-done = bf16[32,40,2048]{2,1,0:T(8,128)(2,1)} async-done(((bf16[32,40,2048]{2,1,0:T(8,128)(2,1)}), bf16[32,40,2048]{2,1,0:T(8,128)(2,1)}, u32[]{:S(2)}, u32[]{:S(2)}) %all-to-all-start) | async-done | bytes 5242912 | tf_op jit(solution)/shard_map/all_to_all | solution.py:19
  198.9 12.0 %gather_fusion = bf16[1024,2048]{1,0:T(8,128)(2,1)} fusion(bf16[1280,2048]{1,0:T(8,128)(2,1)} %bitcast.8, s32[1024]{0:T(1024)S(1)} %broadcast_clamp_fusion), kind=kCustom, calls=%fused_computation | custom fusion | bytes 8392704 | tf_op jit(solution)/shard_map/gather | solution.py:49
  210.9 7.3 %fusion = bf16[128,2048]{1,0:T(8,128)(2,1)} fusion(bf16[1024,2048]{1,0:T(8,128)(2,1)} %gather_fusion, f32[128,8]{1,0:T(8,128)S(1)} %copy.31), kind=kLoop, calls=%fused_computation.3 | loop fusion | flops 6029312 | bytes 4722688 | tf_op jit(solution)/shard_map/reduce_sum | solution.py:51
  (11 shorter events, 0.1 us)
Async XLA Ops:
  6.5 100.5 %copy-start = (bf16[1,768,2048]{2,1,0:T(8,128)(2,1)S(1)}, bf16[1,768,2048]{2,1,0:T(8,128)(2,1)}, u32[]{:S(2)}) copy-start(bf16[1,768,2048]{2,1,0:T(8,128)(2,1)} %param.11) | copy-start | bytes 9437188
  6.5 83.5 %all-gather.2.cloned.1.call-start = ((), (), s32[]{:S(2)}) async-start(), calls=%async_computation.1 | async-start | bytes 17301504 | tf_op jit(solution)/shard_map/all_gather | solution.py:31
  90.0 10.6 %copy-start.4 = (bf16[1,2048,768]{2,1,0:T(8,128)(2,1)S(1)}, bf16[1,2048,768]{2,1,0:T(8,128)(2,1)}, u32[]{:S(2)}) copy-start(bf16[1,2048,768]{2,1,0:T(8,128)(2,1)} %param.10) | copy-start | bytes 9437188
  98.2 2.3 %copy-start.1 = (bf16[32,40,2048]{2,1,0:T(8,128)(2,1)}, bf16[32,40,2048]{2,1,0:T(8,128)(2,1)S(1)}, u32[]{:S(2)}) copy-start(bf16[32,40,2048]{2,1,0:T(8,128)(2,1)S(1)} %convolution_convert_fusion.1) | copy-start | bytes 15728644
  121.7 6.3 %copy-start.2 = (s32[128,8]{0,1:T(8,128)S(1)}, s32[128,8]{0,1:T(8,128)}, u32[]{:S(2)}) copy-start(s32[128,8]{0,1:T(8,128)} %param.7) | copy-start | bytes 12292
  121.7 77.2 %all-to-all-start = ((bf16[32,40,2048]{2,1,0:T(8,128)(2,1)}), bf16[32,40,2048]{2,1,0:T(8,128)(2,1)}, u32[]{:S(2)}, u32[]{:S(2)}) async-start(bf16[32,40,2048]{2,1,0:T(8,128)(2,1)} %convolution_convert_fusion), calls=%async_computation | async-start | bytes 10485760 | tf_op jit(solution)/shard_map/all_to_all | solution.py:19
  128.5 7.5 %copy-start.3 = (s32[128,8]{0,1:T(8,128)S(1)}, s32[128,8]{0,1:T(8,128)}, u32[]{:S(2)}) copy-start(s32[128,8]{0,1:T(8,128)} %param.8) | copy-start | bytes 12292
Sparse Core Ops, SparseCore 0:
  9.9 80.0 all-gather.1
where the time goes:
time: 225 us
  waiting for transfers between devices  121 us (54%)
  matrix products  29.3 us (13%)
  blocking collectives  24.6 us (11%)
  local copies, waits for them, and re-layouts  22.1 us (10%)
  between operations  13.5 us (6%)
  other arithmetic  7.91 us (4%)
  starting transfers between devices  6.25 us (3%)
    all_to_all x1, waiting for transfers between devices, send_back(): lax.all_to_all(outputs, 'expert', split_axis=0, concat_axis=0, tiled=True)  62.8 us
    all_gather x1, waiting for transfers between devices, body(): all_rows = lax.all_gather(tokens, 'expert', axis=0, tiled=True)  57.7 us
    all_gather x1, blocking collectives, body(): all_routes = lax.all_gather(routes, 'expert', axis=0, tiled=True)  24.6 us
    dot_general x1, matrix products, expert_apply(): jnp.einsum('srh,hd->srd', hidden, w_down[0], preferred_element_type=jnp.f...  14.7 us
    gather x1, local copies, waits for them, and re-layouts, body(): picked = returned_flat[flat_slot]  12 us
    dot_general x1, matrix products, body(): jnp.einsum('sct,std->scd', selector, grouped, preferred_element_type=jnp....  8.22 us
    gather x5, local copies, waits for them, and re-layouts, body(): slot_chosen = jnp.take_along_axis(slots, routes, axis=1)  7.39 us
    reduce_sum x1, other arithmetic, body(): combined = jnp.sum(picked.astype(jnp.float32) * weights[:, :, None], axis=1)  7.33 us
  transfers between devices with their start and end apart: 2, of which 2 were waited for; matrix products, arithmetic and copies ran while one was open for 4% of the time, Pallas kernels for 0%

commit v1 on v0

--- a/solution.py
+++ b/solution.py
@@ -28,7 +28,9 @@
     slot_range = jnp.arange(capacity, dtype=jnp.int32)
     onehot = jnp.any(routes[:, :, None] == expert_range[None, None, :], axis=1).astype(jnp.int32)
     slots = jnp.cumsum(onehot, axis=0) - 1
-    all_rows = lax.all_gather(tokens, "expert", axis=0, tiled=True)
+    all_rows = jnp.concatenate(
+        lax.all_to_all(jnp.stack([tokens] * lax.axis_size("expert")), "expert", 0, 0), axis=0
+    )
     all_routes = lax.all_gather(routes, "expert", axis=0, tiled=True)
     own_expert = lax.axis_index("expert")
     routed = (

time: 225 us -> 428 us (1.90)
  blocking collectives: 24.6 us -> 284 us
  waiting for transfers between devices: 121 us -> 63.2 us
  between operations: 13.5 us -> 0.16 us
  starting transfers between devices: 6.25 us -> 13.4 us
  local copies, waits for them, and re-layouts: 22.1 us -> 29.2 us
    all_gather x1, blocking collectives: 24.6 us -> 284 us  [body(): all_routes = lax.all_gather(routes, 'expert', axis=0, tiled=True)]
    all_gather x1 -> x0, waiting for transfers between devices: 57.7 us -> none  [body(): all_rows = lax.all_gather(tokens, 'expert', axis=0, tiled=True)]
    all_to_all x0 -> x1, starting transfers between devices: none -> 7.72 us  [body(): lax.all_to_all(jnp.stack([tokens] * lax.axis_size('expert')), 'expert', 0...]
    another operation x0 -> x1, local copies, waits for them, and re-layouts: none -> 6.94 us  [body(): jnp.stack([tokens] * lax.axis_size('expert'))]
  transfers between devices with their start and end apart: 2 -> 2, of which waited for: 2 -> 1; matrix products, arithmetic and copies ran while one was open for 4% -> 2% of each run, Pallas kernels for 0% -> 0%
where the time goes in v1:
time: 428 us; the launch traced here: 427 us
  blocking collectives  284 us (66%)
  waiting for transfers between devices  63.2 us (15%)
  matrix products  29.3 us (7%)
  local copies, waits for them, and re-layouts  29.2 us (7%)
  starting transfers between devices  13.4 us (3%)
  other arithmetic  7.91 us (2%)
    all_gather x1, blocking collectives, body(): all_routes = lax.all_gather(routes, 'expert', axis=0, tiled=True)  284 us
    all_to_all x1, waiting for transfers between devices, send_back(): lax.all_to_all(outputs, 'expert', split_axis=0, concat_axis=0, tiled=True)  63.2 us
    dot_general x1, matrix products, expert_apply(): jnp.einsum('srh,hd->srd', hidden, w_down[0], preferred_element_type=jnp.f...  14.7 us
    gather x1, local copies, waits for them, and re-layouts, body(): picked = returned_flat[flat_slot]  12.1 us
  transfers between devices with their start and end apart: 2, of which 1 were waited for; matrix products, arithmetic and copies ran while one was open for 2% of the time, Pallas kernels for 0%

profile of v1, /device:TPU:8, one launch (start us, length us, event | category | flops | bytes accessed | tf_op | source)
XLA Modules:
  0.0 427.3 jit_solution(15651454094377053456)
XLA Ops:
  0.0 0.0 copy-start
  0.0 6.9 %stack.2 = bf16[32,128,2048]{2,1,0:T(8,128)(2,1)} broadcast(bf16[128,2048]{1,0:T(8,128)(2,1)} %param.6), dimensions={1,2} | broadcast | bytes 17301504 | tf_op jit(solution)/shard_map/stack | solution.py:32
  6.9 7.7 %all-to-all-start = ((bf16[32,128,2048]{2,1,0:T(8,128)(2,1)}), bf16[32,128,2048]{2,1,0:T(8,128)(2,1)}, u32[]{:S(2)}, u32[]{:S(2)}) async-start(bf16[32,128,2048]{2,1,0:T(8,128)(2,1)} %stack.2), calls=%async_computation | async-start | bytes 33554432 | tf_op jit(solution)/shard_map/all_to_all | solution.py:32
  14.7 0.0 copy-done.3
  14.7 284.1 %all_gather.3 = s32[4096,8]{0,1:T(8,128)S(1)} all-gather(s32[128,8]{0,1:T(8,128)S(1)} %copy-done.3), channel_id=1, replica_groups=mesh['dp'=8,'expert'=32] {'expert'}, dimensions={0}, use_global_device_ids=true | all-gather | bytes 135168 | tf_op jit(solution)/shard_map/all_gather | solution.py:34
  298.8 0.1 compare_reduce_fusion
  298.8 0.3 reduce_window_sum.22
  299.1 0.0 all-to-all-done
  299.1 0.0 copy-start.5
  299.2 8.2 %convolution_convert_fusion.1 = bf16[32,40,2048]{2,1,0:T(8,128)(2,1)S(1)} fusion(bf16[32,128,2048]{2,1,0:T(8,128)(2,1)} %all-to-all-done, s32[32,128]{1,0:T(8,128)S(1)} %broadcast_add_fusion.1, pred[32,128]{1,0:T(8,128)(4,1)S(1)} %broadcast_compare_fusion), kind=kOutput, calls=%fused_computation.5 | convolution fusion | flops 674037760 | bytes 22040576 | tf_op jit(solution)/shard_map/sct,std->scd/dot_general | solution.py:44
  307.4 0.0 copy-start.2
  307.4 2.3 copy-done.2
  309.7 0.0 copy-done.5
  309.7 6.4 %fusion.2 = f32[32,40,768]{2,1,0:T(8,128)} fusion(bf16[32,40,2048]{2,1,0:T(8,128)(2,1)S(1)} %convolution_convert_fusion.1, bf16[1,2048,768]{2,1,0:T(8,128)(2,1)S(1)} %copy-done.5), kind=kOutput, calls=%fused_computation.8 | convolution fusion | flops 4026531840 | bytes 12320768 | tf_op jit(solution)/shard_map/srd,dh->srh/dot_general | solution.py:11
  316.2 0.0 copy-done
  316.2 14.7 %convolution_convert_fusion = bf16[32,40,2048]{2,1,0:T(8,128)(2,1)} fusion(bf16[1,768,2048]{2,1,0:T(8,128)(2,1)S(1)} %copy-done, f32[32,40,768]{2,1,0:T(8,128)} %fusion.2, bf16[32,40,2048]{2,1,0:T(8,128)(2,1)} %copy-done.2, bf16[1,2048,768]{2,1,0:T(8,128)(2,1)} %param.9), kind=kOutput, calls=%fused_computation.4 | convolution fusion | flops 8061583360 | bytes 20709376 | tf_op jit(solution)/shard_map/srh,hd->srd/dot_general | solution.py:13
  330.8 5.6 %all-to-all-start.1 = ((bf16[32,40,2048]{2,1,0:T(8,128)(2,1)}), bf16[32,40,2048]{2,1,0:T(8,128)(2,1)}, u32[]{:S(2)}, u32[]{:S(2)}) async-start(bf16[32,40,2048]{2,1,0:T(8,128)(2,1)} %convolution_convert_fusion), calls=%async_computation.1 | async-start | bytes 10485760 | tf_op jit(solution)/shard_map/all_to_all | solution.py:19
  336.5 0.1 copy.27
  336.6 0.2 reduce_window_sum.23
  336.8 0.1 copy.28
  336.9 0.1 reshape.51
  337.0 0.0 copy-start.4
  337.0 7.1 %gather_fusion.1 = s32[1024]{0:T(1024)S(1)} fusion(s32[128,32]{1,0:T(8,128)S(1)} %broadcast_add_fusion, s32[1024]{0:T(1024)S(1)} %reshape.51), kind=kCustom, calls=%fused_computation.1 | custom fusion | bytes 16384 | tf_op jit(solution)/shard_map/jit(take_along_axis)/gather | solution.py:49
  344.1 0.1 reshape.54
  344.3 0.1 copy.30
  344.4 0.1 reshape.45
  344.5 0.0 copy-done.4
  344.5 0.1 copy.31
  344.6 63.2 %all-to-all-done.1 = bf16[32,40,2048]{2,1,0:T(8,128)(2,1)} async-done(((bf16[32,40,2048]{2,1,0:T(8,128)(2,1)}), bf16[32,40,2048]{2,1,0:T(8,128)(2,1)}, u32[]{:S(2)}, u32[]{:S(2)}) %all-to-all-start.1) | async-done | bytes 5242912 | tf_op jit(solution)/shard_map/all_to_all | solution.py:19
  407.8 12.1 %gather_fusion = bf16[1024,2048]{1,0:T(8,128)(2,1)} fusion(bf16[1280,2048]{1,0:T(8,128)(2,1)} %bitcast.7, s32[1024]{0:T(1024)S(1)} %broadcast_clamp_fusion), kind=kCustom, calls=%fused_computation | custom fusion | bytes 8392704 | tf_op jit(solution)/shard_map/gather | solution.py:51
  420.0 7.3 %fusion = bf16[128,2048]{1,0:T(8,128)(2,1)} fusion(bf16[1024,2048]{1,0:T(8,128)(2,1)} %gather_fusion, f32[128,8]{1,0:T(8,128)S(1)} %copy.31), kind=kLoop, calls=%fused_computation.3 | loop fusion | flops 6029312 | bytes 4722688 | tf_op jit(solution)/shard_map/reduce_sum | solution.py:53
  427.3 0.0 copy-done.1
  (13 shorter events, 0.1 us)
Async XLA Ops:
  0.0 316.2 %copy-start = (bf16[1,768,2048]{2,1,0:T(8,128)(2,1)S(1)}, bf16[1,768,2048]{2,1,0:T(8,128)(2,1)}, u32[]{:S(2)}) copy-start(bf16[1,768,2048]{2,1,0:T(8,128)(2,1)} %param.11) | copy-start | bytes 9437188
  6.9 7.7 %copy-start.3 = (s32[128,8]{0,1:T(8,128)S(1)}, s32[128,8]{0,1:T(8,128)}, u32[]{:S(2)}) copy-start(s32[128,8]{0,1:T(8,128)} %param.7) | copy-start | bytes 12292
  6.9 292.2 %all-to-all-start = ((bf16[32,128,2048]{2,1,0:T(8,128)(2,1)}), bf16[32,128,2048]{2,1,0:T(8,128)(2,1)}, u32[]{:S(2)}, u32[]{:S(2)}) async-start(bf16[32,128,2048]{2,1,0:T(8,128)(2,1)} %stack.2), calls=%async_computation | async-start | bytes 33554432 | tf_op jit(solution)/shard_map/all_to_all | solution.py:32
  299.1 10.6 %copy-start.5 = (bf16[1,2048,768]{2,1,0:T(8,128)(2,1)S(1)}, bf16[1,2048,768]{2,1,0:T(8,128)(2,1)}, u32[]{:S(2)}) copy-start(bf16[1,2048,768]{2,1,0:T(8,128)(2,1)} %param.10) | copy-start | bytes 9437188
  307.4 2.3 copy-start.2
  330.8 77.0 %all-to-all-start.1 = ((bf16[32,40,2048]{2,1,0:T(8,128)(2,1)}), bf16[32,40,2048]{2,1,0:T(8,128)(2,1)}, u32[]{:S(2)}, u32[]{:S(2)}) async-start(bf16[32,40,2048]{2,1,0:T(8,128)(2,1)} %convolution_convert_fusion), calls=%async_computation.1 | async-start | bytes 10485760 | tf_op jit(solution)/shard_map/all_to_all | solution.py:19
  337.0 7.5 %copy-start.4 = (s32[128,8]{0,1:T(8,128)S(1)}, s32[128,8]{0,1:T(8,128)}, u32[]{:S(2)}) copy-start(s32[128,8]{0,1:T(8,128)} %param.8) | copy-start | bytes 12292
  407.8 19.5 %copy-start.1 = (bf16[1,768,2048]{2,1,0:T(8,128)(2,1)S(1)}, bf16[1,768,2048]{2,1,0:T(8,128)(2,1)}, u32[]{:S(2)}) copy-start(bf16[1,768,2048]{2,1,0:T(8,128)(2,1)} %param.11) | copy-start | bytes 9437188
